TPU v7x, 32 devices: a whole 2x2x4 slice. The times are simulated.
32 devices in a mesh: expert: 16 (over z, y, x), replica: 2 (over core).
Axes of the slice: x: 2, y: 2, z: 4, core: 2. Of those that a mesh axis runs over, the one named last changes fastest.
Arguments:
- x_quant: bfloat16 [4096, 2048], P(('expert', 'replica')), may hold values from -6 to 6
- x_scale: float32 [4096, 16], P(('expert', 'replica')), may hold values from 0.3 to 3
- out_grad: bfloat16 [4096, 2048], P(('expert', 'replica')), may hold values from -6 to 6
- expert_ids: int32 [4096, 8], P(('expert', 'replica')), may hold values from 0 to 15, all different within a row; in each aligned block of 128 rows (0 to 127, 128 to 255, ...) at most 80 rows name the same one
- gate_fixed: int32 [4096, 8], P(('expert', 'replica')), may hold values from 1024 to 16383
- w_gate: bfloat16 [16, 2048, 768], P('expert'), may hold values from -0.125 to 0.125
- s_gate: float32 [16, 16, 6], P('expert'), may hold values from 0.3 to 3
- w_up: bfloat16 [16, 2048, 768], P('expert'), may hold values from -0.125 to 0.125
- s_up: float32 [16, 16, 6], P('expert'), may hold values from 0.3 to 3
- w_down: bfloat16 [16, 768, 2048], P('expert'), may hold values from -0.21875 to 0.21875
- s_down: float32 [16, 6, 16], P('expert'), may hold values from 0.3 to 3
Outputs:
- grad_input: bfloat16 [4096, 2048], P(('expert', 'replica'))
- grad_gate: bfloat16 [16, 2048, 768], P('expert', None, 'replica')
- grad_up: bfloat16 [16, 2048, 768], P('expert', None, 'replica')
- grad_down: bfloat16 [16, 768, 2048], P('expert', 'replica')
Inputs may be any that keep to these rules, and one draw needn't show every extreme that they name: `expert_ids`: each row names 8 different experts. Among the rows of one device at most 80 name the same expert, and in every draw some expert is named by exactly 80 rows of some device.
All inputs are finite; a program needn't handle non-finite values.
Results may differ from a plain program's by a relative error of at most 0.012.
Values may be sent and summed in bfloat16 or wider, within the bound.
A program may use at most 192 MiB of HBM per device.

v0:
```python
import jax
import jax.numpy as jnp
from jax import lax
from jax.sharding import PartitionSpec as P


def dequant(weight, scale):
    rows, cols = weight.shape
    srows, scols = scale.shape
    blocks = weight.reshape(srows, rows // srows, scols, cols // scols).astype(jnp.float32)
    return (blocks * scale[:, None, :, None]).reshape(rows, cols).astype(jnp.bfloat16)


def forward_parts(xrows, gate_w, up_w):
    pre_gate = jnp.dot(xrows, gate_w, preferred_element_type=jnp.float32)
    pre_up = jnp.dot(xrows, up_w, preferred_element_type=jnp.float32)
    sig = jax.nn.sigmoid(pre_gate)
    act = pre_gate * sig
    return (pre_gate, pre_up, sig, act)


def unit_grads(row_grad, down_w, pre_gate, pre_up, sig, act):
    hidden_grad = jnp.dot(row_grad, down_w.T, preferred_element_type=jnp.float32)
    up_grad = (hidden_grad * act).astype(jnp.bfloat16)
    gate_grad = (hidden_grad * pre_up * sig * (1.0 + pre_gate * (1.0 - sig))).astype(jnp.bfloat16)
    return (gate_grad, up_grad)


def shards(
    x_quant, x_scale, out_grad, expert_ids, gate_fixed, w_gate, s_gate, w_up, s_up, w_down, s_down
):
    tok_rows, width = x_quant.shape
    topk = expert_ids.shape[1]
    experts = lax.axis_size("expert")
    capacity = tok_rows * topk * 5 // (4 * experts)
    blk_width = width // x_scale.shape[1]
    flat_ids = expert_ids.reshape(-1)
    onehot = (flat_ids[:, None] == jnp.arange(experts, dtype=jnp.int32)[None, :]).astype(jnp.int32)
    before = jnp.cumsum(onehot, axis=0) - onehot
    slot_of = jnp.sum(before * onehot, axis=1)
    token_of = jnp.arange(tok_rows * topk, dtype=jnp.int32) // topk
    table = jnp.full((experts, capacity), tok_rows, jnp.int32).at[flat_ids, slot_of].set(token_of)
    gate_vals = gate_fixed.reshape(-1).astype(jnp.float32) / 65536.0
    gate_table = jnp.zeros((experts, capacity), jnp.float32).at[flat_ids, slot_of].set(gate_vals)
    scaled = x_quant.reshape(tok_rows, -1, blk_width).astype(jnp.float32) * x_scale[:, :, None]
    inputs = scaled.reshape(tok_rows, width).astype(jnp.bfloat16)
    input_pad = jnp.concatenate([inputs, jnp.zeros((1, width), jnp.bfloat16)], axis=0)
    grad_pad = jnp.concatenate([out_grad, jnp.zeros((1, width), jnp.bfloat16)], axis=0)
    send_rows = input_pad[table]
    send_grads = (gate_table[:, :, None] * grad_pad[table].astype(jnp.float32)).astype(jnp.bfloat16)
    got_rows, got_grads = (
        lax.all_to_all(send_rows, "expert", split_axis=0, concat_axis=0, tiled=True),
        lax.all_to_all(send_grads, "expert", split_axis=0, concat_axis=0, tiled=True),
    )
    xrows = got_rows.reshape(experts * capacity, width)
    row_grad = got_grads.reshape(experts * capacity, width)
    gate_w = dequant(w_gate[0], s_gate[0])
    up_w = dequant(w_up[0], s_up[0])
    down_w = dequant(w_down[0], s_down[0])
    pre_gate, pre_up, sig, act = forward_parts(xrows, gate_w, up_w)
    hidden = (act * pre_up).astype(jnp.bfloat16)
    gate_grad, up_grad = unit_grads(row_grad, down_w, pre_gate, pre_up, sig, act)
    row_input = jnp.dot(gate_grad, gate_w.T, preferred_element_type=jnp.float32)
    row_input = row_input + jnp.dot(up_grad, up_w.T, preferred_element_type=jnp.float32)
    term_gate = jnp.dot(xrows.T, gate_grad, preferred_element_type=jnp.float32)
    term_up = jnp.dot(xrows.T, up_grad, preferred_element_type=jnp.float32)
    term_down = jnp.dot(hidden.T, row_grad, preferred_element_type=jnp.float32)
    sum_gate, sum_up, sum_down = (
        lax.psum_scatter(
            term_gate.astype(jnp.bfloat16), "replica", scatter_dimension=1, tiled=True
        ).astype(jnp.float32),
        lax.psum_scatter(
            term_up.astype(jnp.bfloat16), "replica", scatter_dimension=1, tiled=True
        ).astype(jnp.float32),
        lax.psum_scatter(
            term_down.astype(jnp.bfloat16), "replica", scatter_dimension=0, tiled=True
        ).astype(jnp.float32),
    )
    back_rows = row_input.astype(jnp.bfloat16).reshape(experts, capacity, width)
    returned = lax.all_to_all(back_rows, "expert", split_axis=0, concat_axis=0, tiled=True)
    picked = returned[expert_ids, slot_of.reshape(tok_rows, topk)].astype(jnp.float32)
    grad_input = jnp.sum(picked, axis=1).astype(jnp.bfloat16)
    grad_gate = sum_gate.astype(jnp.bfloat16)[None]
    grad_up = sum_up.astype(jnp.bfloat16)[None]
    grad_down = sum_down.astype(jnp.bfloat16)[None]
    return (grad_input, grad_gate, grad_up, grad_down)


def solution(mesh):
    placed = (
        P(("expert", "replica"), None),
        P(("expert", "replica"), None),
        P(("expert", "replica"), None),
        P(("expert", "replica"), None),
        P(("expert", "replica"), None),
        P("expert", None, None),
        P("expert", None, None),
        P("expert", None, None),
        P("expert", None, None),
        P("expert", None, None),
        P("expert", None, None),
    )
    return jax.shard_map(
        shards,
        mesh=mesh,
        in_specs=placed,
        out_specs=(
            P(("expert", "replica"), None),
            P("expert", None, "replica"),
            P("expert", None, "replica"),
            P("expert", "replica", None),
        ),
        check_vma=False,
    )
```

profile of v0, /device:TPU:14, one launch (start us, length us, event | category | flops | bytes accessed | tf_op | source)
XLA Modules:
  0.0 498.3 jit_solution(666598701684857723)
XLA Ops:
  7.2 0.8 copy.48
  8.0 0.1 eq.29
  8.0 0.1 eq.25
  8.1 0.1 reshape.182
  8.3 4.5 reduce-window.6
  12.8 0.1 slice.14
  12.9 0.1 copy.51
  13.1 0.1 broadcast_add_fusion
  13.2 0.6 copy-done.4
  13.8 0.7 multiply_reduce_fusion
  14.6 0.8 and_reduce_fusion
  15.3 4.3 scatter_custom_fusion.1
  19.8 0.8 copy.54
  20.6 0.3 mul.111
  21.0 1.4 fusion.19
  22.4 6.1 %gather_fusion.1 = bf16[1280,2048]{1,0:T(8,128)(2,1)} fusion(bf16[129,2048]{1,0:T(8,128)(2,1)S(1)} %concatenate.15, s32[2048]{0:T(1024)S(1)} %pad_clamp_fusion), kind=kCustom, calls=%fused_computation.1 | custom fusion | bytes 10490880 | tf_op jit(solution)/shard_map/gather | solution.py:49
  28.5 7.3 %all-to-all-start.1 = ((bf16[16,80,2048]{2,1,0:T(8,128)(2,1)}), bf16[16,80,2048]{2,1,0:T(8,128)(2,1)}, u32[]{:S(2)}, u32[]{:S(2)}) async-start(bf16[16,80,2048]{2,1,0:T(8,128)(2,1)} %bitcast.141), calls=%async_computation.1 | async-start | bytes 10485760 | tf_op jit(solution)/shard_map/all_to_all | solution.py:52
  35.9 6.1 %gather_fusion = bf16[1280,2048]{1,0:T(8,128)(2,1)} fusion(bf16[129,2048]{1,0:T(8,128)(2,1)S(1)} %concatenate.14, s32[2048]{0:T(1024)S(1)} %pad_clamp_fusion), kind=kCustom, calls=%fused_computation | custom fusion | bytes 10490880 | tf_op jit(solution)/shard_map/gather | solution.py:50
  42.0 0.1 copy.53
  42.1 0.1 reshape.225
  42.2 4.3 scatter_custom_fusion
  46.6 5.7 %fusion = bf16[16,80,2048]{2,1,0:T(8,128)(2,1)} fusion(bf16[16,80,2048]{2,1,0:T(8,128)(2,1)} %bitcast.142, f32[16,80]{1,0:T(8,128)S(1)} %reshape.191), kind=kLoop, calls=%fused_computation.6 | loop fusion | flops 7864320 | bytes 10490880 | tf_op jit(solution)/shard_map/convert_element_type | solution.py:50
  52.3 101.6 %all-to-all-done.1 = bf16[16,80,2048]{2,1,0:T(8,128)(2,1)} async-done(((bf16[16,80,2048]{2,1,0:T(8,128)(2,1)}), bf16[16,80,2048]{2,1,0:T(8,128)(2,1)}, u32[]{:S(2)}, u32[]{:S(2)}) %all-to-all-start.1) | async-done | bytes 5242912 | tf_op jit(solution)/shard_map/all_to_all | solution.py:52
  153.9 5.4 %all-to-all-start = ((bf16[16,80,2048]{2,1,0:T(8,128)(2,1)}), bf16[16,80,2048]{2,1,0:T(8,128)(2,1)}, u32[]{:S(2)}, u32[]{:S(2)}) async-start(bf16[16,80,2048]{2,1,0:T(8,128)(2,1)} %fusion), calls=%async_computation | async-start | bytes 10485760 | tf_op jit(solution)/shard_map/all_to_all | solution.py:53
  159.3 3.2 copy.56
  162.5 0.8 convert_bitcast_fusion.1
  163.4 0.8 copy-done
  164.2 4.1 copy.74
  168.3 3.6 copy.55
  172.0 0.8 convert_bitcast_fusion.3
  172.8 1.5 copy.72
  174.4 0.4 copy-done.2
  174.7 0.8 convert_bitcast_fusion.4
  175.6 1.5 copy.69
  177.2 0.7 slice-done.1
  177.8 0.6 multiply_convert_fusion
  178.4 0.6 multiply_convert_fusion.1
  179.0 2.2 fusion.5
  181.2 8.7 %fusion.10 = f32[1280,768]{1,0:T(8,128)} fusion(bf16[1280,2048]{1,0:T(8,128)(2,1)} %bitcast.6, bf16[96,8,16,128]{3,2,1,0:T(8,128)(2,1)S(1)} %bitcast.150), kind=kOutput, calls=%fused_computation.31 | convolution fusion | flops 4026531840 | bytes 12320768 | tf_op jit(solution)/shard_map/dot_general | solution.py:15
  190.0 8.8 %fusion.13 = f32[1280,768]{1,0:T(8,128)} fusion(bf16[1280,2048]{1,0:T(8,128)(2,1)} %bitcast.6, bf16[96,8,16,128]{3,2,1,0:T(8,128)(2,1)S(1)} %bitcast.151), kind=kOutput, calls=%fused_computation.34 | convolution fusion | flops 4026531840 | bytes 12320768 | tf_op jit(solution)/shard_map/dot_general | solution.py:16
  198.8 75.8 %all-to-all-done = bf16[16,80,2048]{2,1,0:T(8,128)(2,1)} async-done(((bf16[16,80,2048]{2,1,0:T(8,128)(2,1)}), bf16[16,80,2048]{2,1,0:T(8,128)(2,1)}, u32[]{:S(2)}, u32[]{:S(2)}) %all-to-all-start) | async-done | bytes 5242912 | tf_op jit(solution)/shard_map/all_to_all | solution.py:53
  274.6 12.6 %multiply_convert_fusion.3 = (bf16[1280,768]{1,0:T(8,128)(2,1)}, bf16[1280,768]{1,0:T(8,128)(2,1)S(1)}) fusion(f32[1280,768]{1,0:T(8,128)} %fusion.10, f32[1280,768]{1,0:T(8,128)} %fusion.13, bf16[1280,2048]{1,0:T(8,128)(2,1)} %bitcast.4, bf16[96,8,16,128]{3,2,1,0:T(8,128)(2,1)} %bitcast.149), kind=kOutput, calls=%fused_computation.23 | convolution fusion | flops 4039311360 | bytes 20185088 | tf_op jit(solution)/shard_map/dot_general | solution.py:23
  287.1 1.3 copy-done.11
  288.5 8.4 %convolution_convert_fusion.2 = bf16[2048,768]{1,0:T(8,128)(2,1)} fusion(bf16[1280,2048]{1,0:T(8,128)(2,1)} %bitcast.6, bf16[1280,768]{1,0:T(8,128)(2,1)S(1)} %get-tuple-element.5), kind=kOutput, calls=%fused_computation.29 | convolution fusion | flops 4028104704 | bytes 10354688 | tf_op jit(solution)/shard_map/dot_general | solution.py:65
  296.9 4.7 copy.61
  301.7 9.1 %convolution_convert_fusion.1 = bf16[2048,768]{1,0:T(8,128)(2,1)} fusion(bf16[1280,2048]{1,0:T(8,128)(2,1)} %bitcast.6, bf16[1280,768]{1,0:T(8,128)(2,1)} %get-tuple-element.4), kind=kOutput, calls=%fused_computation.28 | convolution fusion | flops 4028104704 | bytes 10354688 | tf_op jit(solution)/shard_map/dot_general | solution.py:66
  310.8 5.0 %copy.63 = bf16[2048,768]{0,1:T(8,128)(2,1)} copy(bf16[2048,768]{1,0:T(8,128)(2,1)} %convolution_convert_fusion.1) | data formatting | bytes 6291456
  315.8 0.5 mul.119
  316.3 1.4 copy-done.1
  317.7 0.6 copy-done.12
  318.3 8.2 %fusion.7 = f32[1280,2048]{1,0:T(8,128)} fusion(bf16[1280,768]{1,0:T(8,128)(2,1)S(1)} %copy-done.12, bf16[1,2048,768]{1,2,0:T(8,128)(2,1)S(1)} %copy-done.1, f32[96,8,16,128]{3,2,1,0:T(8,128)S(1)} %bitcast.146), kind=kOutput, calls=%fused_computation.30 | convolution fusion | flops 4031250432 | bytes 21889024 | tf_op jit(solution)/shard_map/dot_general | solution.py:63
  326.5 0.5 mul.115
  327.0 1.1 copy-done.13
  328.1 10.1 %add_convert_fusion = bf16[1280,2048]{1,0:T(8,128)(2,1)} fusion(f32[1280,2048]{1,0:T(8,128)} %fusion.7, bf16[1280,768]{1,0:T(8,128)(2,1)S(1)} %copy-done.13, bf16[1,2048,768]{1,2,0:T(8,128)(2,1)S(1)} %copy.55, f32[96,8,16,128]{3,2,1,0:T(8,128)S(1)} %bitcast.145), kind=kOutput, calls=%fused_computation.7 | convolution fusion | flops 4036493312 | bytes 27131904 | tf_op jit(solution)/shard_map/dot_general | solution.py:64
  338.2 5.1 %all-to-all-start.2 = ((bf16[16,80,2048]{2,1,0:T(8,128)(2,1)}), bf16[16,80,2048]{2,1,0:T(8,128)(2,1)}, u32[]{:S(2)}, u32[]{:S(2)}) async-start(bf16[16,80,2048]{2,1,0:T(8,128)(2,1)} %bitcast.147), calls=%async_computation.2 | async-start | bytes 10485760 | tf_op jit(solution)/shard_map/all_to_all | solution.py:80
  343.4 10.9 %convolution_convert_fusion = bf16[768,2048]{1,0:T(8,128)(2,1)} fusion(bf16[1280,2048]{1,0:T(8,128)(2,1)} %bitcast.4, f32[1280,768]{1,0:T(8,128)} %fusion.13, f32[1280,768]{1,0:T(8,128)} %fusion.10), kind=kOutput, calls=%fused_computation.27 | convolution fusion | flops 4034002944 | bytes 16252928 | tf_op jit(solution)/shard_map/dot_general | solution.py:67
  354.3 0.1 reshape.187
  354.5 0.1 copy.60
  354.6 0.1 reshape.217
  354.7 2.8 copy.62
  357.5 2.6 copy.64
  360.1 99.6 %all-to-all-done.2 = bf16[16,80,2048]{2,1,0:T(8,128)(2,1)} async-done(((bf16[16,80,2048]{2,1,0:T(8,128)(2,1)}), bf16[16,80,2048]{2,1,0:T(8,128)(2,1)}, u32[]{:S(2)}, u32[]{:S(2)}) %all-to-all-start.2) | async-done | bytes 5242912 | tf_op jit(solution)/shard_map/all_to_all | solution.py:80
  459.8 25.7 %gather_fusion.2 = bf16[1024,2048]{1,0:T(8,128)(2,1)} fusion(bf16[16,80,2048]{2,1,0:T(8,128)(2,1)} %all-to-all-done.2, s32[1024]{0:T(1024)S(1)} %reshape.217), kind=kCustom, calls=%fused_computation.2 | custom fusion | bytes 8396800 | tf_op jit(solution)/shard_map/gather | solution.py:81
  485.4 5.9 %bitcast_reduce_fusion = bf16[128,2048]{1,0:T(8,128)(2,1)} fusion(bf16[1024,2048]{1,0:T(8,128)(2,1)} %gather_fusion.2), kind=kLoop, calls=%fused_computation.21 | loop fusion | flops 1835008 | bytes 4718592 | tf_op jit(solution)/shard_map/reduce_sum | solution.py:82
  (55 shorter events, 0.8 us)
Async XLA Ops:
  13.2 0.6 copy-start.4
  28.5 7.3 %copy-start.3 = (bf16[128,2048]{1,0:T(8,128)(2,1)S(1)}, bf16[128,2048]{1,0:T(8,128)(2,1)}, u32[]{:S(2)}) copy-start(bf16[128,2048]{1,0:T(8,128)(2,1)} %param.13) | copy-start | bytes 1572868
  28.5 125.3 %all-to-all-start.1 = ((bf16[16,80,2048]{2,1,0:T(8,128)(2,1)}), bf16[16,80,2048]{2,1,0:T(8,128)(2,1)}, u32[]{:S(2)}, u32[]{:S(2)}) async-start(bf16[16,80,2048]{2,1,0:T(8,128)(2,1)} %bitcast.141), calls=%async_computation.1 | async-start | bytes 10485760 | tf_op jit(solution)/shard_map/all_to_all | solution.py:52
  35.9 6.1 %copy-start.7 = (s32[128,8]{0,1:T(8,128)S(1)}, s32[128,8]{0,1:T(8,128)}, u32[]{:S(2)}) copy-start(s32[128,8]{0,1:T(8,128)} %param.15) | copy-start | bytes 12292
  153.9 120.7 %all-to-all-start = ((bf16[16,80,2048]{2,1,0:T(8,128)(2,1)}), bf16[16,80,2048]{2,1,0:T(8,128)(2,1)}, u32[]{:S(2)}, u32[]{:S(2)}) async-start(bf16[16,80,2048]{2,1,0:T(8,128)(2,1)} %fusion), calls=%async_computation | async-start | bytes 10485760 | tf_op jit(solution)/shard_map/all_to_all | solution.py:53
  159.3 195.4 %reduce-scatter.10.cloned.1.call-start = ((), (), s32[]{:S(2)}) async-start(), calls=%async_computation.7 | async-start | bytes 4718592
  162.5 1.7 copy-start
  164.2 4.1 copy-start.8
  172.8 1.5 copy-start.9
  172.8 1.9 copy-start.2
  174.7 2.4 slice-start
  175.6 1.5 copy-start.10
  175.6 2.2 slice-start.1
  287.1 1.3 copy-start.11
  301.6 55.9 %reduce-scatter.12.cloned.1.call-start = ((), (), s32[]{:S(2)}) async-start(), calls=%async_computation.8 | async-start | bytes 4718592
  315.8 1.9 copy-start.1
  315.8 2.5 copy-start.12
  326.5 1.5 copy-start.13
  338.2 121.6 %all-to-all-start.2 = ((bf16[16,80,2048]{2,1,0:T(8,128)(2,1)}), bf16[16,80,2048]{2,1,0:T(8,128)(2,1)}, u32[]{:S(2)}, u32[]{:S(2)}) async-start(bf16[16,80,2048]{2,1,0:T(8,128)(2,1)} %bitcast.147), calls=%async_computation.2 | async-start | bytes 10485760 | tf_op jit(solution)/shard_map/all_to_all | solution.py:80
  343.3 11.0 %copy-start.5 = (s32[1024]{0:T(1024)S(1)}, s32[1024]{0:T(1024)}, u32[]{:S(2)}) copy-start(s32[1024]{0:T(1024)} %copy-done.4) | copy-start | bytes 12292
  343.3 11.1 %copy-start.6 = (s32[128,8]{0,1:T(8,128)S(1)}, s32[128,8]{0,1:T(8,128)}, u32[]{:S(2)}) copy-start(s32[128,8]{0,1:T(8,128)} %param.14) | copy-start | bytes 12292
  343.3 148.0 %reduce-scatter.8.cloned.1.call-start = ((), (), s32[]{:S(2)}) async-start(), calls=%async_computation.6 | async-start | bytes 4718592 | tf_op jit(solution)/shard_map/reduce_scatter | solution.py:75
Sparse Core Ops, SparseCore 0:
  301.7 10.1 reduce-scatter.9
  315.9 10.4 reduce-scatter.11
  354.4 12.0 reduce-scatter.7
where the time goes:
time: 507 us; the launch traced here: 498 us
  waiting for transfers between devices  277 us (55%)
  local copies, waits for them, and re-layouts  86.8 us (17%)
  matrix products  76.9 us (15%)
  other arithmetic  25.1 us (5%)
  starting transfers between devices  17.9 us (4%)
  between operations  14.5 us (3%)
    all_to_all x1, waiting for transfers between devices, shards(): lax.all_to_all(send_rows, 'expert', split_axis=0, concat_axis=0, tiled=True)  102 us
    all_to_all x1, waiting for transfers between devices, shards(): lax.all_to_all(back_rows, 'expert', split_axis=0, concat_axis=0, tiled=True)  99.6 us
    all_to_all x1, waiting for transfers between devices, shards(): lax.all_to_all(send_grads, 'expert', split_axis=0, concat_axis=0, tiled=T...  75.8 us
    unnamed x48, local copies, waits for them, and re-layouts  46.3 us
    gather x1, local copies, waits for them, and re-layouts, shards(): returned[expert_ids, slot_of.reshape(tok_rows, topk)].astype(jnp.float32)  25.7 us
    dot_general x1, matrix products, unit_grads(): jnp.dot(row_grad, down_w.T, preferred_element_type=jnp.float32)  12.6 us
    dot_general x1, matrix products, shards(): term_down = jnp.dot(hidden.T, row_grad, preferred_element_type=jnp.float32)  10.9 us
  transfers between devices with their start and end apart: 6, of which 3 were waited for; matrix products, arithmetic and copies ran while one was open for 27% of the time, Pallas kernels for 0%

commit v1 on v0

v1 whole, which is shorter than its diff:
```python
import jax
import jax.numpy as jnp
from jax import lax
from jax.sharding import PartitionSpec as P


def dequant(weight, scale):
    rows, cols = weight.shape
    srows, scols = scale.shape
    blocks = weight.reshape(srows, rows // srows, scols, cols // scols).astype(jnp.float32)
    return (blocks * scale[:, None, :, None]).reshape(rows, cols).astype(jnp.bfloat16)


def shards(
    x_quant, x_scale, out_grad, expert_ids, gate_fixed, w_gate, s_gate, w_up, s_up, w_down, s_down
):
    f32, bf16 = jnp.float32, jnp.bfloat16
    tok_rows, width = x_quant.shape
    topk = expert_ids.shape[1]
    experts = lax.axis_size("expert")
    capacity = tok_rows * topk * 5 // (4 * experts)
    blk_width = width // x_scale.shape[1]
    scaled = x_quant.reshape(tok_rows, -1, blk_width).astype(f32) * x_scale[:, :, None]
    inputs = scaled.reshape(tok_rows, width).astype(bf16)
    named = expert_ids[None, :, :] == jnp.arange(experts, dtype=jnp.int32)[:, None, None]
    units = jnp.sum(jnp.where(named, gate_fixed[None], 0), axis=2).astype(f32)
    units = lax.all_to_all(units, "expert", split_axis=0, concat_axis=0, tiled=True)
    all_x = lax.all_gather(inputs, "expert", axis=0, tiled=False)
    all_g = lax.all_gather(out_grad, "expert", axis=0, tiled=False)

    chosen = units > 0
    rank = jnp.cumsum(chosen.astype(jnp.int32), axis=1) - 1
    pick = chosen[:, None, :] & (
        rank[:, None, :] == jnp.arange(capacity, dtype=jnp.int32)[None, :, None]
    )
    gates = jnp.sum(jnp.where(pick, units[:, None, :], 0.0), axis=2) / 65536.0
    pick = pick.astype(bf16)

    gate_w = dequant(w_gate[0], s_gate[0])
    up_w = dequant(w_up[0], s_up[0])
    down_w = dequant(w_down[0], s_down[0])
    rows = experts * capacity
    xrows = jnp.einsum("ect,etd->ecd", pick, all_x, preferred_element_type=f32)
    xrows = xrows.astype(bf16).reshape(rows, width)
    row_grad = jnp.einsum("ect,etd->ecd", pick, all_g, preferred_element_type=f32)
    row_grad = (row_grad * gates[:, :, None]).astype(bf16).reshape(rows, width)
    pre_gate = jnp.dot(xrows, gate_w, preferred_element_type=f32)
    pre_up = jnp.dot(xrows, up_w, preferred_element_type=f32)
    sig = jax.nn.sigmoid(pre_gate)
    act = pre_gate * sig
    hidden = (act * pre_up).astype(bf16)
    hidden_grad = jnp.dot(row_grad, down_w.T, preferred_element_type=f32)
    up_grad = (hidden_grad * act).astype(bf16)
    gate_grad = (hidden_grad * pre_up * sig * (1.0 + pre_gate * (1.0 - sig))).astype(bf16)
    row_input = jnp.dot(gate_grad, gate_w.T, preferred_element_type=f32)
    row_input = row_input + jnp.dot(up_grad, up_w.T, preferred_element_type=f32)
    back = row_input.astype(bf16).reshape(experts, capacity, width)
    spread = jnp.einsum("ect,ecd->etd", pick, back, preferred_element_type=f32).astype(bf16)
    grad_input = lax.psum_scatter(
        spread.reshape(experts * tok_rows, width), "expert", scatter_dimension=0, tiled=True
    )
    term_gate = jnp.dot(xrows.T, gate_grad, preferred_element_type=f32).astype(bf16)
    term_up = jnp.dot(xrows.T, up_grad, preferred_element_type=f32).astype(bf16)
    term_down = jnp.dot(hidden.T, row_grad, preferred_element_type=f32).astype(bf16)
    sum_gate = lax.psum_scatter(term_gate, "replica", scatter_dimension=1, tiled=True)
    sum_up = lax.psum_scatter(term_up, "replica", scatter_dimension=1, tiled=True)
    sum_down = lax.psum_scatter(term_down, "replica", scatter_dimension=0, tiled=True)
    return (grad_input, sum_gate[None], sum_up[None], sum_down[None])


def solution(mesh):
    tokens = P(("expert", "replica"), None)
    weights = P("expert", None, None)
    return jax.shard_map(
        shards,
        mesh=mesh,
        in_specs=(tokens,) * 5 + (weights,) * 6,
        out_specs=(
            tokens,
            P("expert", None, "replica"),
            P("expert", None, "replica"),
            P("expert", "replica", None),
        ),
        check_vma=False,
    )
```

time: 507 us -> 509 us (level)
  waiting for transfers between devices: 277 us -> 347 us
  local copies, waits for them, and re-layouts: 86.8 us -> 37.2 us
  other arithmetic: 25.1 us -> 14.5 us
  starting transfers between devices: 17.9 us -> 7.85 us
  matrix products: 76.9 us -> 82 us
    all_to_all x3 -> x1, waiting for transfers between devices: 277 us -> 0.01 us  [shards(): lax.all_to_all(units, 'expert', split_axis=0, concat_axis=0, tiled=True)]
    reduce_scatter x1 -> x2, waiting for transfers between devices: 0.01 us -> 175 us  [the longest x1 175 us: shards(): lax.psum_scatter(spread.reshape(experts * tok_rows, width), 'expert', sca...]
    all_gather x0 -> x2, waiting for transfers between devices: none -> 172 us  [the longest x1 96.1 us: shards(): all_g = lax.all_gather(out_grad, 'expert', axis=0, tiled=False)]
    gather x3 -> x0, local copies, waits for them, and re-layouts: 37.9 us -> none  [the longest x1 25.7 us: shards(): returned[expert_ids, slot_of.reshape(tok_rows, topk)].astype(jnp.float32)]
    all_to_all x3 -> x1, starting transfers between devices: 17.8 us -> 7.14 us  [shards(): lax.all_to_all(units, 'expert', split_axis=0, concat_axis=0, tiled=True)]
    unnamed x48 -> x51, local copies, waits for them, and re-layouts: 46.3 us -> 35.9 us
    reduce_sum x2, other arithmetic: 5.91 us -> 0.39 us  [the longest x1 0.36 us: shards(): gates = jnp.sum(jnp.where(pick, units[:, None, :], 0.0), axis=2) / 65536.0]
    dot_general x8 -> x11, matrix products: 76.9 us -> 82 us  [the longest x1 10.9 us: shards(): jnp.dot(hidden.T, row_grad, preferred_element_type=f32).astype(bf16)]
  transfers between devices with their start and end apart: 6 -> 7, of which waited for: 3 -> 3; matrix products, arithmetic and copies ran while one was open for 27% -> 20% of each run, Pallas kernels for 0% -> 0%
where the time goes in v1:
time: 509 us; the launch traced here: 503 us
  waiting for transfers between devices  347 us (68%)
  matrix products  82 us (16%)
  local copies, waits for them, and re-layouts  37.2 us (7%)
  between operations  14.7 us (3%)
  other arithmetic  14.5 us (3%)
  starting transfers between devices  7.85 us (2%)
    reduce_scatter x1, waiting for transfers between devices, shards(): lax.psum_scatter(spread.reshape(experts * tok_rows, width), 'expert', sca...  175 us
    all_gather x1, waiting for transfers between devices, shards(): all_g = lax.all_gather(out_grad, 'expert', axis=0, tiled=False)  96.1 us
    all_gather x1, waiting for transfers between devices, shards(): all_x = lax.all_gather(inputs, 'expert', axis=0, tiled=False)  75.5 us
    unnamed x51, local copies, waits for them, and re-layouts  35.9 us
    dot_general x1, matrix products, shards(): jnp.dot(hidden.T, row_grad, preferred_element_type=f32).astype(bf16)  10.9 us
    dot_general x1, matrix products, shards(): hidden_grad = jnp.dot(row_grad, down_w.T, preferred_element_type=f32)  10.2 us
  transfers between devices with their start and end apart: 7, of which 3 were waited for; matrix products, arithmetic and copies ran while one was open for 20% of the time, Pallas kernels for 0%

profile of v1, /device:TPU:14, one launch (start us, length us, event | category | flops | bytes accessed | tf_op | source)
XLA Modules:
  0.0 503.4 jit_solution(18409121597189280319)
XLA Ops:
  7.2 0.0 copy-start.8
  7.2 0.0 all-gather.7.cloned.1.call-start
  7.2 0.8 copy.38
  8.0 0.3 mul.107
  8.4 2.2 fusion.18
  10.5 0.0 all-gather.7.cloned.1.call-update
  10.6 0.0 all-gather.5.cloned.1.call-start
  10.6 0.7 all-gather.5.cloned.1.call-update
  11.4 0.6 convert_element_type.145
  12.0 7.1 %all-to-all-start = ((f32[16,1,128]{2,1,0:T(1,128)}), f32[16,1,128]{2,1,0:T(1,128)S(1)}, u32[]{:S(2)}, u32[]{:S(2)}) async-start(f32[16,1,128]{2,1,0:T(1,128)} %bitcast.1), calls=%async_computation | async-start | bytes 16384 | tf_op jit(solution)/shard_map/all_to_all | solution.py:27
  19.1 0.0 reduce-scatter.13.cloned.1.call-start
  19.2 3.3 copy.39
  22.4 0.8 convert_bitcast_fusion.3
  23.3 0.0 copy-start.9
  23.3 4.1 copy.51
  27.4 5.3 %copy.40 = bf16[1,2048,768]{1,2,0:T(8,128)(2,1)} copy(bf16[1,2048,768]{2,1,0:T(8,128)(2,1)} %param.16) | data formatting | bytes 6291456 | tf_op args[5]
  32.7 2.7 convert_bitcast_fusion.1
  35.4 0.0 copy-start.10
  35.4 0.0 copy-start.3
  35.4 1.5 copy.53
  37.0 0.4 copy-done.3
  37.3 0.8 convert_bitcast_fusion.4
  38.2 0.0 copy-start.11
  38.2 0.0 slice-start.1
  38.2 1.5 copy.48
  39.8 0.7 slice-done.1
  40.4 2.2 multiply_convert_fusion.2
  42.6 2.2 multiply_convert_fusion.1
  44.8 2.2 fusion.4
  47.1 0.0 all-to-all-done
  47.1 0.3 reduce_window_sum.14
  47.4 0.4 select_reduce_fusion
  47.7 75.5 %all-gather.7.cloned.1.call-done = bf16[2048,2048]{1,0:T(8,128)(2,1)} async-done(((bf16[128,2048]{1,0:T(8,128)(2,1)}), bf16[2048,2048]{1,0:T(8,128)(2,1)}) %all-gather.7.cloned.1.call-update) | async-done | bytes 8388624 | tf_op jit(solution)/shard_map/all_gather | solution.py:28
  123.2 5.0 %convolution_convert_fusion.1 = bf16[16,80,2048]{2,1,0:T(8,128)(2,1)S(1)} fusion(bf16[16,128,2048]{2,1,0:T(8,128)(2,1)} %bitcast.122, s32[16,128]{1,0:T(8,128)S(1)} %broadcast_add_fusion, pred[16,128]{1,0:T(8,128)(4,1)S(1)} %get-tuple-element.5), kind=kOutput, calls=%fused_computation.16 | convolution fusion | flops 674037760 | bytes 13641728 | tf_op jit(solution)/shard_map/ect,etd->ecd/dot_general | solution.py:43
  128.3 6.2 %fusion.12 = f32[1280,768]{1,0:T(8,128)} fusion(bf16[1280,2048]{1,0:T(8,128)(2,1)S(1)} %bitcast.130, bf16[96,8,16,128]{3,2,1,0:T(8,128)(2,1)S(1)} %bitcast.143), kind=kOutput, calls=%fused_computation.29 | convolution fusion | flops 4026531840 | bytes 12320768 | tf_op jit(solution)/shard_map/dot_general | solution.py:48
  134.5 6.4 %fusion.9 = f32[1280,768]{1,0:T(8,128)} fusion(bf16[1280,2048]{1,0:T(8,128)(2,1)S(1)} %bitcast.131, bf16[96,8,16,128]{3,2,1,0:T(8,128)(2,1)S(1)} %bitcast.144), kind=kOutput, calls=%fused_computation.26 | convolution fusion | flops 4026531840 | bytes 12320768 | tf_op jit(solution)/shard_map/dot_general | solution.py:47
  140.9 96.1 %all-gather.5.cloned.1.call-done = bf16[2048,2048]{1,0:T(8,128)(2,1)} async-done(((bf16[128,2048]{1,0:T(8,128)(2,1)}), bf16[2048,2048]{1,0:T(8,128)(2,1)}) %all-gather.5.cloned.1.call-update) | async-done | bytes 8388624 | tf_op jit(solution)/shard_map/all_gather | solution.py:29
  237.1 5.0 %multiply_convert_fusion = bf16[16,80,2048]{2,1,0:T(8,128)(2,1)S(1)} fusion(f32[16,80]{1,0:T(8,128)S(1)} %broadcast_multiply_fusion, bf16[16,128,2048]{2,1,0:T(8,128)(2,1)} %bitcast.121, s32[16,128]{1,0:T(8,128)S(1)} %broadcast_add_fusion, pred[16,128]{1,0:T(8,128)(4,1)S(1)} %get-tuple-element.5), kind=kOutput, calls=%fused_computation.1 | convolution fusion | flops 676659200 | bytes 13646848 | tf_op jit(solution)/shard_map/ect,etd->ecd/dot_general | solution.py:45
  242.1 0.4 copy-done.14
  242.5 10.2 %multiply_convert_fusion.4 = (bf16[1280,768]{1,0:T(8,128)(2,1)}, bf16[1280,768]{1,0:T(8,128)(2,1)S(1)}) fusion(f32[1280,768]{1,0:T(8,128)} %fusion.9, f32[1280,768]{1,0:T(8,128)S(1)} %copy-done.14, bf16[1280,2048]{1,0:T(8,128)(2,1)S(1)} %bitcast.128, bf16[96,8,16,128]{3,2,1,0:T(8,128)(2,1)S(1)} %bitcast.142), kind=kOutput, calls=%fused_computation.18 | convolution fusion | flops 4039311360 | bytes 20185088 | tf_op jit(solution)/shard_map/dot_general | solution.py:52
  252.7 1.3 copy-done.12
  254.0 5.8 %convolution_convert_fusion.4 = bf16[2048,768]{1,0:T(8,128)(2,1)} fusion(bf16[1280,2048]{1,0:T(8,128)(2,1)S(1)} %bitcast.135, bf16[1280,768]{1,0:T(8,128)(2,1)S(1)} %get-tuple-element.7), kind=kOutput, calls=%fused_computation.24 | convolution fusion | flops 4028104704 | bytes 10354688 | tf_op jit(solution)/shard_map/dot_general | solution.py:62
  259.8 4.7 copy.41
  264.5 0.0 reduce-scatter.13.cloned.1.call-update
  264.5 0.3 reduce-scatter.15.cloned.1.call-start
  264.8 9.2 %convolution_convert_fusion.3 = bf16[2048,768]{1,0:T(8,128)(2,1)} fusion(bf16[1280,2048]{1,0:T(8,128)(2,1)} %bitcast.132, bf16[1280,768]{1,0:T(8,128)(2,1)} %get-tuple-element.6), kind=kOutput, calls=%fused_computation.23 | convolution fusion | flops 4028104704 | bytes 10354688 | tf_op jit(solution)/shard_map/dot_general | solution.py:63
  273.9 4.8 copy.43
  278.8 0.0 reduce-scatter.15.cloned.1.call-update
  278.8 0.0 reduce-scatter.11.cloned.1.call-start
  278.9 10.9 %convolution_convert_fusion.2 = bf16[768,2048]{1,0:T(8,128)(2,1)} fusion(bf16[1280,2048]{1,0:T(8,128)(2,1)} %bitcast.129, f32[1280,768]{1,0:T(8,128)} %fusion.12, f32[1280,768]{1,0:T(8,128)} %fusion.9), kind=kOutput, calls=%fused_computation.22 | convolution fusion | flops 4034002944 | bytes 16252928 | tf_op jit(solution)/shard_map/dot_general | solution.py:64
  289.7 0.0 reduce-scatter.11.cloned.1.call-update
  289.7 0.3 reduce-scatter.9.cloned.1.call-start
  290.1 0.5 mul.115
  290.5 1.4 copy-done.2
  292.0 0.6 copy-done.13
  292.6 8.2 %fusion.6 = f32[1280,2048]{1,0:T(8,128)} fusion(bf16[1280,768]{1,0:T(8,128)(2,1)S(1)} %copy-done.13, bf16[1,2048,768]{1,2,0:T(8,128)(2,1)S(1)} %copy-done.2, f32[96,8,16,128]{3,2,1,0:T(8,128)S(1)} %bitcast.139), kind=kOutput, calls=%fused_computation.25 | convolution fusion | flops 4031250432 | bytes 21889024 | tf_op jit(solution)/shard_map/dot_general | solution.py:55
  300.8 0.5 mul.111
  301.3 9.5 %add_convert_fusion = bf16[1280,2048]{1,0:T(8,128)(2,1)S(1)} fusion(f32[1280,2048]{1,0:T(8,128)} %fusion.6, bf16[1280,768]{1,0:T(8,128)(2,1)} %get-tuple-element.6, bf16[1,2048,768]{1,2,0:T(8,128)(2,1)S(1)} %copy.39, f32[96,8,16,128]{3,2,1,0:T(8,128)S(1)} %bitcast.138), kind=kOutput, calls=%fused_computation | convolution fusion | flops 4036493312 | bytes 27131904 | tf_op jit(solution)/shard_map/dot_general | solution.py:56
  310.8 5.6 %convolution_convert_fusion = bf16[16,128,2048]{2,1,0:T(8,128)(2,1)} fusion(bf16[16,80,2048]{2,1,0:T(8,128)(2,1)S(1)} %bitcast.140, s32[16,128]{1,0:T(8,128)S(1)} %broadcast_add_fusion, pred[16,128]{1,0:T(8,128)(4,1)S(1)} %get-tuple-element.5), kind=kOutput, calls=%fused_computation.15 | convolution fusion | flops 675610624 | bytes 13641728 | tf_op jit(solution)/shard_map/ect,ecd->etd/dot_general | solution.py:58
  316.4 0.0 reduce-scatter.9.cloned.1.call-update
  316.4 0.0 reduce-scatter.13.cloned.1.call-done
  316.5 2.6 copy.42
  319.0 2.6 copy.44
  321.6 174.7 %reduce-scatter.9.cloned.1.call-done = bf16[128,2048]{1,0:T(8,128)(2,1)} async-done(((bf16[2048,2048]{1,0:T(8,128)(2,1)}), bf16[128,2048]{1,0:T(8,128)(2,1)}) %reduce-scatter.9.cloned.1.call-update) | async-done | bytes 524304 | tf_op jit(solution)/shard_map/reduce_scatter | solution.py:59
  (37 shorter events, 0.1 us)
Async XLA Ops:
  7.2 4.2 copy-start.8
  7.2 4.2 copy-start.7
  7.2 116.1 %all-gather.7.cloned.1.call-start = ((), (), s32[]{:S(2)}) async-start(), calls=%async_computation.8 | async-start | bytes 8912896 | tf_op jit(solution)/shard_map/all_gather | solution.py:28
  10.6 226.5 %all-gather.5.cloned.1.call-start = ((), (), s32[]{:S(2)}) async-start(), calls=%async_computation.7 | async-start | bytes 8912896 | tf_op jit(solution)/shard_map/all_gather | solution.py:29
  12.0 35.1 %all-to-all-start = ((f32[16,1,128]{2,1,0:T(1,128)}), f32[16,1,128]{2,1,0:T(1,128)S(1)}, u32[]{:S(2)}, u32[]{:S(2)}) async-start(f32[16,1,128]{2,1,0:T(1,128)} %bitcast.1), calls=%async_computation | async-start | bytes 16384 | tf_op jit(solution)/shard_map/all_to_all | solution.py:27
  19.1 297.3 %reduce-scatter.13.cloned.1.call-start = ((), (), s32[]{:S(2)}) async-start(), calls=%async_computation.9 | async-start | bytes 4718592
  23.3 4.1 copy-start.9
  35.4 1.5 copy-start.10
  35.4 1.9 copy-start.3
  37.3 2.4 slice-start
  38.2 1.5 copy-start.11
  38.2 2.2 slice-start.1
  123.2 5.1 %copy-start.5 = (bf16[16,128,6,128]{1,0,3,2:T(8,128)(2,1)S(1)}, bf16[16,128,6,128]{1,0,3,2:T(8,128)(2,1)}, u32[]{:S(2)}) copy-start(bf16[16,128,6,128]{1,0,3,2:T(8,128)(2,1)} %multiply_convert_fusion.2) | copy-start | bytes 9437188
  128.3 6.2 %copy-start.1 = (bf16[16,80,2048]{2,1,0:T(8,128)(2,1)}, bf16[16,80,2048]{2,1,0:T(8,128)(2,1)S(1)}, u32[]{:S(2)}) copy-start(bf16[16,80,2048]{2,1,0:T(8,128)(2,1)S(1)} %convolution_convert_fusion.1) | copy-start | bytes 15728644
  128.3 6.2 %copy-start.6 = (bf16[16,128,6,128]{1,0,3,2:T(8,128)(2,1)S(1)}, bf16[16,128,6,128]{1,0,3,2:T(8,128)(2,1)}, u32[]{:S(2)}) copy-start(bf16[16,128,6,128]{1,0,3,2:T(8,128)(2,1)} %multiply_convert_fusion.1) | copy-start | bytes 9437188
  237.1 5.1 %copy-start.4 = (bf16[6,128,16,128]{3,2,1,0:T(8,128)(2,1)S(1)}, bf16[6,128,16,128]{3,2,1,0:T(8,128)(2,1)}, u32[]{:S(2)}) copy-start(bf16[6,128,16,128]{3,2,1,0:T(8,128)(2,1)} %fusion.4) | copy-start | bytes 9437188
  237.1 5.5 %copy-start.14 = (f32[1280,768]{1,0:T(8,128)S(1)}, f32[1280,768]{1,0:T(8,128)}, u32[]{:S(2)}) copy-start(f32[1280,768]{1,0:T(8,128)} %fusion.12) | copy-start | bytes 11796484
  237.1 16.9 %slice-start.2 = ((s8[5242880]{0:T(1024)(128)(4,1)}), s8[4194304]{0:T(1024)(128)(4,1)S(1)}, s32[]{:S(2)}) async-start(s8[5242880]{0:T(1024)(128)(4,1)} %bitcast.133), calls=%async_computation.13 | async-start | bytes 8388608
  242.1 10.6 %copy-start = (bf16[16,80,2048]{2,1,0:T(8,128)(2,1)}, bf16[16,80,2048]{2,1,0:T(8,128)(2,1)S(1)}, u32[]{:S(2)}) copy-start(bf16[16,80,2048]{2,1,0:T(8,128)(2,1)S(1)} %multiply_convert_fusion) | copy-start | bytes 15728644
  242.5 11.5 %slice-start.3 = ((s8[5242880]{0:T(1024)(128)(4,1)}), s8[1048576]{0:T(1024)(128)(4,1)S(1)}, s32[]{:S(2)}) async-start(s8[5242880]{0:T(1024)(128)(4,1)} %bitcast.133), calls=%async_computation.14 | async-start | bytes 2097152
  252.7 1.3 copy-start.12
  264.5 54.5 %reduce-scatter.15.cloned.1.call-start = ((), (), s32[]{:S(2)}) async-start(), calls=%async_computation.10 | async-start | bytes 4718592
  278.8 42.8 %reduce-scatter.11.cloned.1.call-start = ((), (), s32[]{:S(2)}) async-start(), calls=%async_computation.6 | async-start | bytes 4718592 | tf_op jit(solution)/shard_map/reduce_scatter | solution.py:67
  289.7 206.6 %reduce-scatter.9.cloned.1.call-start = ((), (), s32[]{:S(2)}) async-start(), calls=%async_computation.5 | async-start | bytes 8912896 | tf_op jit(solution)/shard_map/reduce_scatter | solution.py:59
  290.1 1.9 copy-start.2
  290.1 2.5 copy-start.13
Sparse Core Ops, SparseCore 0:
  11.4 111.8 all-gather.6
  126.0 111.0 all-gather.4
  264.7 11.4 reduce-scatter.12
  278.9 11.4 reduce-scatter.14
  293.1 12.0 reduce-scatter.10
  316.5 179.7 reduce-scatter.8
